TPU v7x, 32 devices: a whole 2x2x4 slice. The times are simulated.
32 devices in a mesh: dp: 2 (over x), expert: 16 (over z, y, core).
Axes of the slice: x: 2, y: 2, z: 4, core: 2. Of those that a mesh axis runs over, the one named last changes fastest.
Arguments:
- tokens: bfloat16 [4096, 1024], P(('dp', 'expert')), may hold values from -6 to 6
- grad_out: bfloat16 [4096, 1024], P(('dp', 'expert')), may hold values from -6 to 6
- expert_ids: int32 [4096, 8], P(('dp', 'expert')), may hold values from 0 to 15, all different within a row; in each aligned block of 128 rows (0 to 127, 128 to 255, ...) at most 72 rows name the same one
- gates: float32 [4096, 8], P(('dp', 'expert')), may hold values from 0.1 to 0.5
- w_in: bfloat16 [16, 1024, 768], P('expert', 'dp'), may hold values from -0.1875 to 0.1875
- w_down: bfloat16 [16, 384, 1024], P('expert', 'dp'), may hold values from -0.3125 to 0.3125
Outputs:
- grad_tokens: bfloat16 [4096, 1024], P(('dp', 'expert'))
- grad_in: float32 [16, 1024, 768], P('expert', 'dp')
- grad_down: float32 [16, 384, 1024], P('expert', 'dp')
Inputs may be any that keep to these rules, and one draw needn't show every extreme that they name: `expert_ids`: each token names 8 different experts; among the tokens of one device no expert is named more than 72 times, a bound that some block reaches.
All inputs are finite; a program needn't handle non-finite values.
Results may differ from a plain program's by a relative error of at most 0.015.
Values may be sent and summed in bfloat16 or wider, within the bound.
A program may use at most 64 MiB of HBM per device.

v0:
```python
import jax
import jax.numpy as jnp
from jax import lax
from jax.sharding import PartitionSpec as P


def hidden_from(preact):
    half_width = preact.shape[1] // 2
    gate_pre = preact[:, :half_width]
    up_pre = preact[:, half_width:]
    sigmoid_gate = jax.nn.sigmoid(gate_pre)
    return (gate_pre * sigmoid_gate * up_pre).astype(jnp.bfloat16)


def pre_grads(preact, grad_hidden):
    half_width = preact.shape[1] // 2
    gate_pre = preact[:, :half_width]
    up_pre = preact[:, half_width:]
    sigmoid_gate = jax.nn.sigmoid(gate_pre)
    grad_gate = grad_hidden * up_pre * sigmoid_gate * (1.0 + gate_pre * (1.0 - sigmoid_gate))
    grad_up = grad_hidden * gate_pre * sigmoid_gate
    return jnp.concatenate([grad_gate, grad_up], axis=1).astype(jnp.bfloat16)


def contract_first(left, right):
    return lax.dot_general(
        left, right, (((0,), (0,)), ((), ())), preferred_element_type=jnp.float32
    )


def contract_last(left, right):
    return lax.dot_general(
        left, right, (((1,), (1,)), ((), ())), preferred_element_type=jnp.float32
    )


def on_device(tokens, grad_out, expert_ids, gates, w_in, w_down):
    token_rows, model_width = tokens.shape
    route_width = expert_ids.shape[1]
    expert_count = lax.axis_size("expert")
    route_total = token_rows * route_width
    capacity = route_total // expert_count + max(1, route_total // (8 * expert_count))
    slot_total = expert_count * capacity
    flat_ids = expert_ids.reshape(route_total)
    route_marks = (flat_ids[:, None] == jnp.arange(expert_count, dtype=jnp.int32)[None, :]).astype(
        jnp.int32
    )
    route_index = jnp.arange(route_total, dtype=jnp.int32)
    lower_table = (route_index[None, :] <= route_index[:, None]).astype(jnp.bfloat16)
    running = jnp.dot(
        lower_table, route_marks.astype(jnp.bfloat16), preferred_element_type=jnp.float32
    )
    slot_ranks = jnp.sum((running.astype(jnp.int32) - 1) * route_marks, axis=1)
    targets = flat_ids * capacity + slot_ranks
    route_of_slot = jnp.full((slot_total,), route_total, jnp.int32).at[targets].set(route_index)
    occupied = route_of_slot < route_total
    clipped = jnp.minimum(route_of_slot, route_total - 1)
    source_rows = clipped // route_width
    slot_gates = jnp.where(
        occupied, gates.reshape(route_total)[clipped], jnp.zeros((), jnp.float32)
    )
    send_tokens = jnp.where(occupied[:, None], tokens[source_rows], jnp.zeros((), jnp.bfloat16))
    send_grads = (slot_gates[:, None] * grad_out[source_rows].astype(jnp.float32)).astype(
        jnp.bfloat16
    )
    recv_tokens, recv_grads = (
        lax.all_to_all(
            send_tokens.reshape(expert_count, capacity, model_width),
            "expert",
            split_axis=0,
            concat_axis=0,
            tiled=True,
        ),
        lax.all_to_all(
            send_grads.reshape(expert_count, capacity, model_width),
            "expert",
            split_axis=0,
            concat_axis=0,
            tiled=True,
        ),
    )
    slot_tokens = recv_tokens.reshape(slot_total, model_width)
    slot_grads = recv_grads.reshape(slot_total, model_width)
    local_in = w_in[0]
    local_down = w_down[0]
    full_in, full_down = (
        lax.all_gather(local_in, "dp", axis=0, tiled=True),
        lax.all_gather(local_down, "dp", axis=0, tiled=True),
    )
    preact = jnp.dot(slot_tokens, full_in, preferred_element_type=jnp.float32)
    grad_hidden = contract_last(slot_grads, full_down)
    pre_grad = pre_grads(preact, grad_hidden)
    slot_back = contract_last(pre_grad, full_in).astype(jnp.bfloat16)
    hidden_act = hidden_from(preact)
    columns = slot_tokens
    grad_in_local = lax.psum_scatter(
        contract_first(columns, pre_grad).astype(jnp.bfloat16),
        "dp",
        scatter_dimension=0,
        tiled=True,
    ).astype(jnp.float32)
    columns = hidden_act
    grad_down_local = lax.psum_scatter(
        contract_first(columns, slot_grads).astype(jnp.bfloat16),
        "dp",
        scatter_dimension=0,
        tiled=True,
    ).astype(jnp.float32)
    slot_return = lax.all_to_all(
        slot_back.reshape(expert_count, capacity, model_width),
        "expert",
        split_axis=0,
        concat_axis=0,
        tiled=True,
    )
    per_route = slot_return.reshape(slot_total, model_width)[targets]
    grad_tokens = jnp.sum(
        per_route.reshape(token_rows, route_width, model_width).astype(jnp.float32), axis=1
    ).astype(jnp.bfloat16)
    return (grad_tokens, grad_in_local[None], grad_down_local[None])


def solution(mesh):
    in_specs = (
        P(("dp", "expert"), None),
        P(("dp", "expert"), None),
        P(("dp", "expert"), None),
        P(("dp", "expert"), None),
        P("expert", "dp", None),
        P("expert", "dp", None),
    )
    out_specs = (P(("dp", "expert"), None), P("expert", "dp", None), P("expert", "dp", None))
    return jax.shard_map(
        on_device, mesh=mesh, in_specs=in_specs, out_specs=out_specs, check_vma=False
    )
```

profile of v0, /device:TPU:13, one launch (start us, length us, event | category | flops | bytes accessed | tf_op | source)
XLA Modules:
  0.0 228.2 jit_solution(2143589263287731506)
XLA Ops:
  7.2 0.0 copy-start
  7.2 0.8 copy.10
  8.0 0.7 broadcast_multiply_fusion
  8.7 0.1 eq.15
  8.8 0.5 fusion.8
  9.3 0.1 copy.9
  9.4 0.1 mul.56
  9.5 4.3 %scatter_custom_fusion = s32[1152]{0:T(1024)S(1)} fusion(s32[1024]{0:T(1024)S(1)} %bitcast.37, s32[1024]{0:T(1024)S(1)} %iota.13, s32[]{:T(128)} %constant.13.clone.1), kind=kCustom, calls=%fused_computation.47 | custom fusion | bytes 4612 | tf_op jit(solution)/shard_map/scatter | solution.py:55
  13.9 0.8 copy.11
  14.7 0.1 reshape.72
  14.8 4.6 %gather_fusion = f32[1152]{0:T(1024)S(1)} fusion(f32[1024]{0:T(1024)S(1)} %reshape.72, s32[2048]{0:T(1024)S(1)} %get-tuple-element.10), kind=kCustom, calls=%fused_computation | custom fusion | bytes 13824 | tf_op jit(solution)/shard_map/gather | solution.py:60
  19.4 0.1 broadcast_in_dim.47
  19.4 0.0 copy-done
  19.5 4.4 %gather_fusion.2 = bf16[1152,1024]{1,0:T(8,128)(2,1)S(1)} fusion(bf16[128,1024]{1,0:T(8,128)(2,1)S(1)} %copy-done, s32[2048]{0:T(1024)S(1)} %get-tuple-element.9), kind=kCustom, calls=%fused_computation.2 | custom fusion | bytes 4723200 | tf_op jit(solution)/shard_map/gather | solution.py:62
  23.8 1.7 broadcast_select_fusion
  25.5 6.7 %all-to-all-start.1 = ((bf16[16,72,1024]{2,1,0:T(8,128)(2,1)}), bf16[16,72,1024]{2,1,0:T(8,128)(2,1)}, u32[]{:S(2)}, u32[]{:S(2)}) async-start(bf16[16,72,1024]{2,1,0:T(8,128)(2,1)} %broadcast_select_fusion), calls=%async_computation.1 | async-start | bytes 4718592 | tf_op jit(solution)/shard_map/all_to_all | solution.py:67
  32.2 0.1 mul.58
  32.3 0.0 copy-done.1
  32.3 4.4 %gather_fusion.1 = bf16[1152,1024]{1,0:T(8,128)(2,1)S(1)} fusion(bf16[128,1024]{1,0:T(8,128)(2,1)S(1)} %copy-done.1, s32[2048]{0:T(1024)S(1)} %get-tuple-element.9), kind=kCustom, calls=%fused_computation.1 | custom fusion | bytes 4723200 | tf_op jit(solution)/shard_map/gather | solution.py:63
  36.7 1.9 fusion
  38.5 46.8 %all-to-all-done.1 = bf16[16,72,1024]{2,1,0:T(8,128)(2,1)} async-done(((bf16[16,72,1024]{2,1,0:T(8,128)(2,1)}), bf16[16,72,1024]{2,1,0:T(8,128)(2,1)}, u32[]{:S(2)}, u32[]{:S(2)}) %all-to-all-start.1) | async-done | bytes 2359328 | tf_op jit(solution)/shard_map/all_to_all | solution.py:67
  85.3 4.9 %all-to-all-start = ((bf16[16,72,1024]{2,1,0:T(8,128)(2,1)}), bf16[16,72,1024]{2,1,0:T(8,128)(2,1)S(1)}, u32[]{:S(2)}, u32[]{:S(2)}) async-start(bf16[16,72,1024]{2,1,0:T(8,128)(2,1)} %fusion), calls=%async_computation | async-start | bytes 4718592 | tf_op jit(solution)/shard_map/all_to_all | solution.py:74
  90.2 0.0 all-gather.4.cloned.1.call-start
  90.3 0.7 all-gather.4.cloned.1.call-update
  91.0 0.0 reduce-scatter.5.cloned.1.call-start
  91.0 11.2 %all-gather = bf16[1,384,1024]{2,1,0:T(8,128)(2,1)S(1)} all-gather(bf16[1,192,1024]{2,1,0:T(8,128)(2,1)} %param.11), channel_id=2, replica_groups=mesh['dp'=2,'expert'=16] {'dp'}, dimensions={1}, use_global_device_ids=true | all-gather | bytes 1179648 | tf_op jit(solution)/shard_map/all_gather | solution.py:88
  102.2 18.2 %all-gather.4.cloned.1.call-done = bf16[1,1024,768]{2,1,0:T(8,128)(2,1)} async-done(((bf16[1,512,768]{2,1,0:T(8,128)(2,1)}), bf16[1,1024,768]{2,1,0:T(8,128)(2,1)}) %all-gather.4.cloned.1.call-update) | async-done | bytes 1572880 | tf_op jit(solution)/shard_map/all_gather | solution.py:87
  120.4 6.1 %fusion.3 = f32[1152,768]{0,1:T(8,128)} fusion(bf16[1152,1024]{1,0:T(8,128)(2,1)} %bitcast.6, bf16[1,1024,768]{2,1,0:T(8,128)(2,1)} %all-gather.4.cloned.1.call-done), kind=kOutput, calls=%fused_computation.19 | convolution fusion | flops 1811939328 | bytes 7471104 | tf_op jit(solution)/shard_map/dot_general | solution.py:90
  126.5 16.7 %all-to-all-done = bf16[16,72,1024]{2,1,0:T(8,128)(2,1)S(1)} async-done(((bf16[16,72,1024]{2,1,0:T(8,128)(2,1)}), bf16[16,72,1024]{2,1,0:T(8,128)(2,1)S(1)}, u32[]{:S(2)}, u32[]{:S(2)}) %all-to-all-start) | async-done | bytes 2359328 | tf_op jit(solution)/shard_map/all_to_all | solution.py:74
  143.3 4.1 %convolution_convert_fusion.2 = bf16[384,1024]{1,0:T(8,128)(2,1)} fusion(bf16[1152,1024]{1,0:T(8,128)(2,1)S(1)} %bitcast.34, f32[1152,768]{0,1:T(8,128)} %fusion.3), kind=kOutput, calls=%fused_computation.21 | convolution fusion | flops 909017088 | bytes 6684672 | tf_op jit(solution)/shard_map/dot_general | solution.py:26
  147.4 0.0 reduce-scatter.5.cloned.1.call-update
  147.4 0.0 copy-start.2
  147.4 3.7 %multiply_convert_fusion.2 = (bf16[1152,384]{0,1:T(8,128)(2,1)S(1)}, bf16[1152,384]{0,1:T(8,128)(2,1)S(1)}) fusion(f32[1152,768]{0,1:T(8,128)} %fusion.3, bf16[1152,1024]{1,0:T(8,128)(2,1)S(1)} %bitcast.35, bf16[1,384,1024]{2,1,0:T(8,128)(2,1)S(1)} %all-gather), kind=kOutput, calls=%fused_computation.15 | convolution fusion | flops 911720448 | bytes 8454144 | tf_op jit(solution)/shard_map/dot_general | solution.py:32
  151.1 0.0 copy-start.3
  151.1 0.0 copy-start.4
  151.1 3.5 %convolution_convert_fusion = bf16[1152,1024]{1,0:T(8,128)(2,1)} fusion(bf16[1,1024,768]{2,1,0:T(8,128)(2,1)S(1)} %copy-done.2, bf16[1152,384]{0,1:T(8,128)(2,1)S(1)} %get-tuple-element.6, bf16[1152,384]{0,1:T(8,128)(2,1)S(1)} %get-tuple-element.5), kind=kOutput, calls=%fused_computation.9 | convolution fusion | flops 1816657920 | bytes 5701632 | tf_op jit(solution)/shard_map/dot_general | solution.py:32
  154.6 0.0 copy-done.3
  154.6 4.9 %all-to-all-start.2 = ((bf16[16,72,1024]{2,1,0:T(8,128)(2,1)}), bf16[16,72,1024]{2,1,0:T(8,128)(2,1)S(1)}, u32[]{:S(2)}, u32[]{:S(2)}) async-start(bf16[16,72,1024]{2,1,0:T(8,128)(2,1)} %bitcast.36), calls=%async_computation.2 | async-start | bytes 4718592 | tf_op jit(solution)/shard_map/all_to_all | solution.py:109
  159.5 0.0 reduce-scatter.3.cloned.1.call-start
  159.5 5.6 %convolution_convert_fusion.1 = bf16[1024,768]{1,0:T(8,128)(2,1)} fusion(bf16[1152,1024]{1,0:T(8,128)(2,1)} %bitcast.6, bf16[1152,384]{0,1:T(8,128)(2,1)} %copy-done.4, bf16[1152,384]{0,1:T(8,128)(2,1)} %copy-done.3), kind=kOutput, calls=%fused_computation.17 | convolution fusion | flops 1816264704 | bytes 5701632 | tf_op jit(solution)/shard_map/dot_general | solution.py:26
  165.1 0.0 reduce-scatter.3.cloned.1.call-update
  165.2 0.0 reduce-scatter.5.cloned.1.call-done
  165.2 2.0 bitcast_convert_fusion.1
  167.1 26.3 %reduce-scatter.3.cloned.1.call-done = bf16[512,768]{1,0:T(8,128)(2,1)} async-done(((bf16[1024,768]{1,0:T(8,128)(2,1)}), bf16[512,768]{1,0:T(8,128)(2,1)}) %reduce-scatter.3.cloned.1.call-update) | async-done | bytes 786448 | tf_op jit(solution)/shard_map/reduce_scatter | solution.py:96
  193.5 2.4 %bitcast_convert_fusion = f32[1,512,768]{2,1,0:T(8,128)} fusion(bf16[512,768]{1,0:T(8,128)(2,1)} %reduce-scatter.3.cloned.1.call-done), kind=kLoop, calls=%fused_computation.26 | loop fusion | flops 393216 | bytes 2359296 | tf_op jit(solution)/shard_map/broadcast_in_dim | solution.py:120
  195.9 16.7 %all-to-all-done.2 = bf16[16,72,1024]{2,1,0:T(8,128)(2,1)S(1)} async-done(((bf16[16,72,1024]{2,1,0:T(8,128)(2,1)}), bf16[16,72,1024]{2,1,0:T(8,128)(2,1)S(1)}, u32[]{:S(2)}, u32[]{:S(2)}) %all-to-all-start.2) | async-done | bytes 2359328 | tf_op jit(solution)/shard_map/all_to_all | solution.py:109
  212.5 5.4 %gather_fusion.3 = bf16[1024,1024]{1,0:T(8,128)(2,1)} fusion(bf16[1152,1024]{1,0:T(8,128)(2,1)S(1)} %bitcast.31, s32[1024]{0:T(1024)S(1)} %broadcast_clamp_fusion), kind=kCustom, calls=%fused_computation.3 | custom fusion | bytes 4198400 | tf_op jit(solution)/shard_map/gather | solution.py:116
  217.9 3.7 %bitcast_reduce_fusion = bf16[128,1024]{1,0:T(8,128)(2,1)} fusion(bf16[1024,1024]{1,0:T(8,128)(2,1)} %gather_fusion.3), kind=kLoop, calls=%fused_computation.11 | loop fusion | flops 917504 | bytes 2359296 | tf_op jit(solution)/shard_map/reduce_sum | solution.py:117
  (9 shorter events, 0.1 us)
Async XLA Ops:
  7.2 12.3 %copy-start = (bf16[128,1024]{1,0:T(8,128)(2,1)S(1)}, bf16[128,1024]{1,0:T(8,128)(2,1)}, u32[]{:S(2)}) copy-start(bf16[128,1024]{1,0:T(8,128)(2,1)} %param.6) | copy-start | bytes 786436
  25.5 6.8 %copy-start.1 = (bf16[128,1024]{1,0:T(8,128)(2,1)S(1)}, bf16[128,1024]{1,0:T(8,128)(2,1)}, u32[]{:S(2)}) copy-start(bf16[128,1024]{1,0:T(8,128)(2,1)} %param.7) | copy-start | bytes 786436
  25.5 59.8 %all-to-all-start.1 = ((bf16[16,72,1024]{2,1,0:T(8,128)(2,1)}), bf16[16,72,1024]{2,1,0:T(8,128)(2,1)}, u32[]{:S(2)}, u32[]{:S(2)}) async-start(bf16[16,72,1024]{2,1,0:T(8,128)(2,1)} %broadcast_select_fusion), calls=%async_computation.1 | async-start | bytes 4718592 | tf_op jit(solution)/shard_map/all_to_all | solution.py:67
  85.3 57.9 %all-to-all-start = ((bf16[16,72,1024]{2,1,0:T(8,128)(2,1)}), bf16[16,72,1024]{2,1,0:T(8,128)(2,1)S(1)}, u32[]{:S(2)}, u32[]{:S(2)}) async-start(bf16[16,72,1024]{2,1,0:T(8,128)(2,1)} %fusion), calls=%async_computation | async-start | bytes 4718592 | tf_op jit(solution)/shard_map/all_to_all | solution.py:74
  90.2 30.2 %all-gather.4.cloned.1.call-start = ((), (), s32[]{:S(2)}) async-start(), calls=%async_computation.7 | async-start | bytes 2359296 | tf_op jit(solution)/shard_map/all_gather | solution.py:87
  91.0 74.2 %reduce-scatter.5.cloned.1.call-start = ((), (), s32[]{:S(2)}) async-start(), calls=%async_computation.6 | async-start | bytes 1179648 | tf_op jit(solution)/shard_map/reduce_scatter | solution.py:103
  147.4 3.7 %copy-start.2 = (bf16[1,1024,768]{2,1,0:T(8,128)(2,1)S(1)}, bf16[1,1024,768]{2,1,0:T(8,128)(2,1)}, u32[]{:S(2)}) copy-start(bf16[1,1024,768]{2,1,0:T(8,128)(2,1)} %all-gather.4.cloned.1.call-done) | copy-start | bytes 4718596
  151.1 3.5 %copy-start.3 = (bf16[1152,384]{0,1:T(8,128)(2,1)}, bf16[1152,384]{0,1:T(8,128)(2,1)S(1)}, u32[]{:S(2)}) copy-start(bf16[1152,384]{0,1:T(8,128)(2,1)S(1)} %get-tuple-element.5) | copy-start | bytes 2654212
  151.1 3.5 %copy-start.4 = (bf16[1152,384]{0,1:T(8,128)(2,1)}, bf16[1152,384]{0,1:T(8,128)(2,1)S(1)}, u32[]{:S(2)}) copy-start(bf16[1152,384]{0,1:T(8,128)(2,1)S(1)} %get-tuple-element.6) | copy-start | bytes 2654212
  154.6 57.9 %all-to-all-start.2 = ((bf16[16,72,1024]{2,1,0:T(8,128)(2,1)}), bf16[16,72,1024]{2,1,0:T(8,128)(2,1)S(1)}, u32[]{:S(2)}, u32[]{:S(2)}) async-start(bf16[16,72,1024]{2,1,0:T(8,128)(2,1)} %bitcast.36), calls=%async_computation.2 | async-start | bytes 4718592 | tf_op jit(solution)/shard_map/all_to_all | solution.py:109
  159.5 34.0 %reduce-scatter.3.cloned.1.call-start = ((), (), s32[]{:S(2)}) async-start(), calls=%async_computation.5 | async-start | bytes 2359296 | tf_op jit(solution)/shard_map/reduce_scatter | solution.py:96
Sparse Core Ops, SparseCore 0:
  92.6 27.7 all-gather.3
  147.5 16.8 reduce-scatter.4
  167.4 26.0 reduce-scatter.2
where the time goes:
time: 229 us; the launch traced here: 228 us
  waiting for transfers between devices  125 us (55%)
  local copies, waits for them, and re-layouts  25.2 us (11%)
  matrix products  23.4 us (10%)
  starting transfers between devices  16.6 us (7%)
  between operations  13.9 us (6%)
  other arithmetic  12.3 us (5%)
  blocking collectives  11.2 us (5%)
    all_to_all x1, waiting for transfers between devices, on_device(): lax.all_to_all(send_tokens.reshape(expert_count, capacity, model_width),...  46.8 us
    reduce_scatter x1, waiting for transfers between devices, on_device(): lax.psum_scatter(contract_first(columns, pre_grad).astype(jnp.bfloat16),...  26.3 us
    all_gather x1, waiting for transfers between devices, on_device(): lax.all_gather(local_in, 'dp', axis=0, tiled=True)  18.2 us
    all_to_all x1, waiting for transfers between devices, on_device(): lax.all_to_all(send_grads.reshape(expert_count, capacity, model_width), '...  16.7 us
    all_to_all x1, waiting for transfers between devices, on_device(): lax.all_to_all(slot_back.reshape(expert_count, capacity, model_width), 'e...  16.7 us
    all_gather x1, blocking collectives, on_device(): lax.all_gather(local_down, 'dp', axis=0, tiled=True)  11.2 us
    dot_general x2, matrix products, contract_first(): lax.dot_general(left, right, (((0,), (0,)), ((), ())), preferred_element_...  9.69 us
    dot_general x2, matrix products, contract_last(): lax.dot_general(left, right, (((1,), (1,)), ((), ())), preferred_element_...  7.13 us
  transfers between devices with their start and end apart: 6, of which 5 were waited for; matrix products, arithmetic and copies ran while one was open for 13% of the time, Pallas kernels for 0%

commit v1 on v0

--- a/solution.py
+++ b/solution.py
@@ -1,7 +1,16 @@
+import functools
+
 import jax
 import jax.numpy as jnp
 from jax import lax
+from jax.experimental import pallas as pl
+from jax.experimental.pallas import tpu as pltpu
 from jax.sharding import PartitionSpec as P
+
+MESH = pl.DeviceIdType.MESH
+F32 = jnp.float32
+BF16 = jnp.bfloat16
+VMEM_BYTES = 56 * 1024 * 1024
 
 
 def hidden_from(preact):
@@ -120,6 +129,385 @@
     return (grad_tokens, grad_in_local[None], grad_down_local[None])
 
 
+def fused_kernel(
+    expert_count, capacity,
+    ids_ref, gates_ref, tok_in, grad_in, win_in, wdn_in,
+    gtok_out, gin_out, gdn_out,
+    data, meta, win, wdn, acc_in, acc_dn, sel, xs, gs, act, dpre, part,
+    sib_in, y_out, y_in, z_out, z_in, gin_send, gin_recv, gdn_send, gdn_recv,
+    local_sem, own_send, fwd_send, y_send, sib_send, recv_sem,
+    w_send, w_recv, sib_part_send, sib_part_recv, y_part_send, y_part_recv,
+    z_part_send, z_part_recv, g_send, g_recv,
+):
+    depth = expert_count // 4
+    dp = lax.axis_index("dp")
+    me = lax.axis_index("expert")
+    z, y, c = me // 4, (me // 2) % 2, me % 2
+    token_rows, model_width = tok_in.shape
+    half_in, half_dn = win_in.shape[0], wdn_in.shape[0]
+    half_width = wdn.shape[0]
+    slots = 4 * capacity
+    tile = model_width // 4
+
+    def block_of(zz, yy, cc):
+        return zz * 4 + yy * 2 + cc
+
+    sib, y_peer = block_of(z, y, 1 - c), block_of(z, 1 - y, c)
+    table = [sorted(range(depth), key=lambda b: (abs(b - zz), b)) for zz in range(depth)]
+
+    def near(k):
+        total = jnp.int32(0)
+        for zz in range(depth):
+            for kk in range(depth):
+                hit = (z == zz).astype(jnp.int32) * (jnp.int32(k) == kk).astype(jnp.int32)
+                total = total + hit * table[zz][kk]
+        return total
+
+    def data_copy(block, target, sems):
+        return (
+            pltpu.make_async_remote_copy(
+                src_ref=data.at[block], dst_ref=data.at[block],
+                send_sem=sems.at[0], recv_sem=recv_sem.at[block, 0],
+                device_id=(dp, target), device_id_type=MESH),
+            pltpu.make_async_remote_copy(
+                src_ref=meta.at[block], dst_ref=meta.at[block],
+                send_sem=sems.at[1], recv_sem=recv_sem.at[block, 1],
+                device_id=(dp, target), device_id_type=MESH),
+        )
+
+    def ship(block, target, sems):
+        for copy in data_copy(block, target, sems):
+            copy.start()
+
+    def sent(block, target, sems):
+        for copy in data_copy(block, target, sems):
+            copy.wait_send()
+
+    def arrived(block):
+        for copy in data_copy(block, sib, own_send.at[0]):
+            copy.wait_recv()
+
+    own_rows_in = pl.ds(pl.multiple_of(dp * half_in, 16), half_in)
+    own_rows_dn = pl.ds(pl.multiple_of(dp * half_dn, 16), half_dn)
+    peer_rows_dn = pl.ds(pl.multiple_of((1 - dp) * half_dn, 16), half_dn)
+    local = [
+        pltpu.make_async_copy(tok_in, data.at[me, 0], local_sem.at[0]),
+        pltpu.make_async_copy(grad_in, data.at[me, 1], local_sem.at[1]),
+        pltpu.make_async_copy(win_in, win.at[own_rows_in], local_sem.at[2]),
+        pltpu.make_async_copy(wdn_in, wdn.at[own_rows_dn], local_sem.at[3]),
+    ]
+    for copy in local:
+        copy.start()
+
+    barrier = pltpu.get_barrier_semaphore()
+    partners = [(dp, sib), (dp, y_peer), (1 - dp, me)]
+    for step in range(1, depth):
+        partners.append((dp, block_of((z + step) % depth, y, c)))
+    for partner in partners:
+        pl.semaphore_signal(barrier, inc=1, device_id=partner, device_id_type=MESH)
+
+    experts = lax.broadcasted_iota(jnp.int32, (expert_count, token_rows), 0)
+    marks = jnp.zeros((expert_count, token_rows), F32)
+    scale = jnp.zeros((expert_count, token_rows), F32)
+    for k in range(ids_ref.shape[0]):
+        hit = ids_ref[k : k + 1, :] == experts
+        marks = marks + jnp.where(hit, 1.0, 0.0)
+        scale = scale + jnp.where(hit, gates_ref[k : k + 1, :], 0.0)
+    before = (
+        lax.broadcasted_iota(jnp.int32, (token_rows, token_rows), 0)
+        < lax.broadcasted_iota(jnp.int32, (token_rows, token_rows), 1)
+    )
+    ranks = jnp.dot(
+        marks.astype(BF16), jnp.where(before, 1.0, 0.0).astype(BF16), preferred_element_type=F32
+    )
+    meta[me, 0:expert_count, :] = jnp.where(marks > 0.5, ranks, -1.0)
+    meta[me, expert_count : 2 * expert_count, :] = scale
+
+    pl.semaphore_wait(barrier, len(partners))
+
+    weights = [
+        pltpu.make_async_remote_copy(
+            src_ref=src, dst_ref=dst, send_sem=w_send.at[i], recv_sem=w_recv.at[i],
+            device_id=(1 - dp, me), device_id_type=MESH)
+        for i, (src, dst) in enumerate(
+            ((win_in, win.at[own_rows_in]), (wdn_in, wdn.at[own_rows_dn])))
+    ]
+    local[0].wait()
+    local[1].wait()
+
+    @pl.when(z > 0)
+    def _():
+        ship(me, block_of(jnp.maximum(z - 1, 0), y, c), own_send.at[0])
+
+    @pl.when(z < depth - 1)
+    def _():
+        ship(me, block_of(jnp.minimum(z + 1, depth - 1), y, c), own_send.at[1])
+
+    ship(me, y_peer, y_send.at[0])
+    for copy in weights:
+        copy.start()
+    ship(me, sib, sib_send.at[0, 0])
+
+    def onward(zz):
+        step_to = jnp.where(zz < z, z + 1, z - 1)
+        return (step_to >= 0) & (step_to < depth), jnp.clip(step_to, 0, depth - 1)
+
+    def arrivals(k):
+        zz = near(k)
+        block = block_of(zz, y, c)
+        arrived(block)
+        more, step_to = onward(zz)
+
+        @pl.when(more)
+        def _():
+            ship(block, block_of(step_to, y, c), fwd_send.at[k])
+
+        ship(block, y_peer, y_send.at[k])
+        ship(block, sib, sib_send.at[k, 0])
+
+    def sib_part(k):
+        return pltpu.make_async_remote_copy(
+            src_ref=part.at[k, 1 - c], dst_ref=sib_in.at[k],
+            send_sem=sib_part_send.at[k], recv_sem=sib_part_recv.at[k],
+            device_id=(dp, sib), device_id_type=MESH)
+
+    def y_part(k):
+        return pltpu.make_async_remote_copy(
+            src_ref=y_out.at[k], dst_ref=y_in.at[k],
+            send_sem=y_part_send.at[k], recv_sem=y_part_recv.at[k],
+            device_id=(dp, y_peer), device_id_type=MESH)
+
+    def z_part(k, slot):
+        return pltpu.make_async_remote_copy(
+            src_ref=z_out.at[k], dst_ref=z_in.at[slot],
+            send_sem=z_part_send.at[k], recv_sem=z_part_recv.at[slot],
+            device_id=(dp, block_of(near(k), y, c)), device_id_type=MESH)
+
+    def gin_part(i):
+        rows = pl.ds(pl.multiple_of(i * tile, tile), tile)
+        return pltpu.make_async_remote_copy(
+            src_ref=gin_send.at[rows], dst_ref=gin_recv.at[rows],
+            send_sem=g_send.at[i], recv_sem=g_recv.at[i],
+            device_id=(1 - dp, me), device_id_type=MESH)
+
+    half_tiles = half_in // tile
+    gdn_part = pltpu.make_async_remote_copy(
+        src_ref=gdn_send, dst_ref=gdn_recv,
+        send_sem=g_send.at[half_tiles], recv_sem=g_recv.at[half_tiles],
+        device_id=(1 - dp, me), device_id_type=MESH)
+
+    def combine_y(k):
+        sib_part(k).wait_recv()
+        y_out[k] = (
+            part[k, c, 1 - y].astype(F32) + sib_in[k, 1 - y].astype(F32)
+        ).astype(BF16)
+        y_part(k).start()
+
+    def combine_z(k):
+        y_part(k).wait_recv()
+        z_out[k] = (
+            part[k, c, y].astype(F32) + sib_in[k, y].astype(F32) + y_in[k].astype(F32)
+        ).astype(BF16)
+
+        @pl.when(k > 0)
+        def _():
+            z_part(jnp.maximum(k, 1), z).start()
+
+    acc_in[...] = jnp.zeros_like(acc_in)
+    acc_dn[...] = jnp.zeros_like(acc_dn)
+    for k in range(1, min(3, depth)):
+        arrivals(k)
+    local[2].wait()
+    local[3].wait()
+
+    def chunk(k, carry):
+        @pl.when((k >= 1) & (k + 2 < depth))
+        def _():
+            arrivals(jnp.minimum(k + 2, depth - 1))
+
+        zz = near(k)
+        block = block_of(zz, 1 - y, c)
+        arrived(block)
+        ship(block, sib, sib_send.at[k, 1])
+        arrived(block_of(zz, y, 1 - c))
+        arrived(block_of(zz, 1 - y, 1 - c))
+
+        @pl.when(k == 0)
+        def _():
+            for copy in weights:
+                copy.wait_recv()
+
+        first = zz * 4
+        slot_rows = lax.broadcasted_iota(jnp.int32, (slots, token_rows), 0)
+        slot_gate = jnp.zeros((slots, 1), F32)
+        for j in range(4):
+            rank = meta[first + j, pl.ds(me, 1), :].astype(jnp.int32)
+            place = jnp.where(rank >= 0, rank + j * capacity, -1)
+            scale_row = meta[first + j, pl.ds(expert_count + me, 1), :]
+            hit = slot_rows == place
+            slot_gate = slot_gate + jnp.sum(
+                jnp.where(hit, scale_row, 0.0), axis=1, keepdims=True
+            )
+            sel[:, j * token_rows : (j + 1) * token_rows] = jnp.where(hit, 1.0, 0.0).astype(BF16)
+        chosen = sel[...]
+        chunk_tokens = data[pl.ds(first, 4), 0].reshape(4 * token_rows, model_width)
+        xs[...] = jnp.dot(chosen, chunk_tokens, preferred_element_type=F32).astype(BF16)
+        chunk_grads = data[pl.ds(first, 4), 1].reshape(4 * token_rows, model_width)
+        gs[...] = (
+            slot_gate * jnp.dot(chosen, chunk_grads, preferred_element_type=F32)
+        ).astype(BF16)
+        preact = jnp.dot(xs[...], win[...], preferred_element_type=F32)
+        grad_hidden = contract_last(gs[...], wdn[...])
+        act[...] = hidden_from(preact)
+        dpre[...] = pre_grads(preact, grad_hidden)
+
+        last = k == depth - 1
+
+        @pl.loop(0, 4)
+        def _(i):
+            at = ((1 - dp) * half_tiles + i) % 4
+            rows = pl.ds(pl.multiple_of(at * tile, tile), tile)
+            total = acc_in[rows, :] + contract_first(xs[:, rows], dpre[...])
+            acc_in[rows, :] = total
+
+            @pl.when(last & (i < half_tiles))
+            def _():
+                piece = jnp.minimum(i, half_tiles - 1)
+                gin_send[pl.ds(pl.multiple_of(piece * tile, tile), tile), :] = total.astype(BF16)
+                gin_part(piece).start()
+
+        acc_dn[...] += contract_first(act[...], gs[...])
+
+        @pl.when(last)
+        def _():
+            gdn_send[...] = acc_dn[peer_rows_dn, :].astype(BF16)
+            gdn_part.start()
+
+        back = contract_last(dpre[...], win[...]).astype(BF16)
+        spread = contract_first(sel[...], back).astype(BF16)
+        for j in range(4):
+            part[k, j % 2, j // 2] = spread[j * token_rows : (j + 1) * token_rows]
+        sib_part(k).start()
+
+        @pl.when(k >= 1)
+        def _():
+            combine_y(jnp.maximum(k - 1, 0))
+
+        @pl.when(k >= 2)
+        def _():
+            combine_z(jnp.maximum(k - 2, 0))
+
+        return carry
+
+    lax.fori_loop(0, depth, chunk, 0)
+    combine_y(depth - 1)
+    if depth >= 2:
+        combine_z(jnp.int32(depth - 2))
+    combine_z(jnp.int32(depth - 1))
+
+    total = z_out[0].astype(F32)
+    for step in range(1, depth):
+        slot = (z + step) % depth
+        z_part(step, slot).wait_recv()
+        total = total + z_in[slot].astype(F32)
+    gtok_out[...] = total.astype(BF16)
+
+    for i in range(half_tiles):
+        gin_part(i).wait_recv()
+        rows = pl.ds(i * tile, tile)
+        own = pl.ds(pl.multiple_of(dp * half_in + i * tile, tile), tile)
+        gin_out[rows, :] = acc_in[own, :].astype(BF16).astype(F32) + gin_recv[rows, :].astype(F32)
+    gdn_part.wait_recv()
+    gdn_out[...] = acc_dn[own_rows_dn, :].astype(BF16).astype(F32) + gdn_recv[...].astype(F32)
+
+    @pl.when(z > 0)
+    def _():
+        sent(me, sib, own_send.at[0])
+
+    @pl.when(z < depth - 1)
+    def _():
+        sent(me, sib, own_send.at[1])
+
+    for k in range(depth):
+        sent(me, y_peer, y_send.at[k])
+        sent(me, sib, sib_send.at[k, 0])
+        sent(me, sib, sib_send.at[k, 1])
+        sib_part(k).wait_send()
+        y_part(k).wait_send()
+        if k > 0:
+            more, _ = onward(near(k))
+
+            @pl.when(more)
+            def _():
+                sent(me, sib, fwd_send.at[k])
+
+            z_part(k, z).wait_send()
+    for copy in weights:
+        copy.wait_send()
+    for i in range(half_tiles):
+        gin_part(i).wait_send()
+    gdn_part.wait_send()
+
+
+def fused_on_device(tokens, grad_out, expert_ids, gates, w_in, w_down):
+    token_rows, model_width = tokens.shape
+    route_total = token_rows * expert_ids.shape[1]
+    expert_count = lax.axis_size("expert")
+    capacity = route_total // expert_count + max(1, route_total // (8 * expert_count))
+    depth = expert_count // 4
+    slots = 4 * capacity
+    half_in, in_width = w_in.shape[1:]
+    half_dn = w_down.shape[1]
+    half_tiles = half_in // (model_width // 4)
+    dma = lambda *shape: pltpu.SemaphoreType.DMA(shape)
+    vmem = lambda shape, dtype=BF16: pltpu.VMEM(shape, dtype)
+    grad_tokens, grad_in, grad_down = pl.pallas_call(
+        functools.partial(fused_kernel, expert_count, capacity),
+        out_shape=(
+            jax.ShapeDtypeStruct((token_rows, model_width), BF16),
+            jax.ShapeDtypeStruct((half_in, in_width), F32),
+            jax.ShapeDtypeStruct((half_dn, model_width), F32),
+        ),
+        in_specs=[pl.BlockSpec(memory_space=pltpu.VMEM)] * 2
+        + [pl.BlockSpec(memory_space=pl.ANY)] * 4,
+        out_specs=(pl.BlockSpec(memory_space=pltpu.VMEM),) * 3,
+        scratch_shapes=[
+            vmem((expert_count, 2, token_rows, model_width)),
+            vmem((expert_count, 2 * expert_count, token_rows), F32),
+            vmem((2 * half_in, in_width)),
+            vmem((2 * half_dn, model_width)),
+            vmem((2 * half_in, in_width), F32),
+            vmem((2 * half_dn, model_width), F32),
+            vmem((slots, 4 * token_rows)),
+            vmem((slots, model_width)),
+            vmem((slots, model_width)),
+            vmem((slots, in_width // 2)),
+            vmem((slots, in_width)),
+            vmem((depth, 2, 2, token_rows, model_width)),
+            vmem((depth, 2, token_rows, model_width)),
+            vmem((depth, token_rows, model_width)),
+            vmem((depth, token_rows, model_width)),
+            vmem((depth, token_rows, model_width)),
+            vmem((depth, token_rows, model_width)),
+            vmem((half_in, in_width)),
+            vmem((half_in, in_width)),
+            vmem((half_dn, model_width)),
+            vmem((half_dn, model_width)),
+            dma(4), dma(2, 2), dma(depth, 2), dma(depth, 2), dma(depth, 2, 2),
+            dma(expert_count, 2), dma(2), dma(2), dma(depth), dma(depth), dma(depth), dma(depth),
+            dma(depth), dma(depth), dma(half_tiles + 1), dma(half_tiles + 1),
+        ],
+        compiler_params=pltpu.CompilerParams(
+            collective_id=0, has_side_effects=True, vmem_limit_bytes=VMEM_BYTES
+        ),
+    )(expert_ids.T, gates.T, tokens, grad_out, w_in[0], w_down[0])
+    return grad_tokens, grad_in[None], grad_down[None]
+
+
+def fits_fused(mesh):
+    return mesh.shape["dp"] == 2 and mesh.shape["expert"] in (8, 16)
+
+
 def solution(mesh):
     in_specs = (
         P(("dp", "expert"), None),
@@ -131,5 +519,6 @@
     )
     out_specs = (P(("dp", "expert"), None), P("expert", "dp", None), P("expert", "dp", None))
     return jax.shard_map(
-        on_device, mesh=mesh, in_specs=in_specs, out_specs=out_specs, check_vma=False
-    )
+        fused_on_device if fits_fused(mesh) else on_device,
+        mesh=mesh, in_specs=in_specs, out_specs=out_specs, check_vma=False
+    )

time: 229 us -> 108 us (0.47)
  the two profiles are of different devices: /device:TPU:13 before, /device:TPU:0 now
where the time goes in v1:
time: 108 us
  Pallas kernels  102 us (94%)
  local copies, waits for them, and re-layouts  5.28 us (5%)
    pallas_call x1, Pallas kernels, fused_on_device(): pl.pallas_call(functools.partial(fused_kernel, expert_count, capacity), o...  102 us
    unnamed x5, local copies, waits for them, and re-layouts  5.28 us

profile of v1, /device:TPU:0, one launch (start us, length us, event | category | flops | bytes accessed | tf_op | source)
XLA Modules:
  0.0 107.5 jit_solution(5089395684441670995)
XLA Ops:
  0.6 101.6 %shard_map.85 = (bf16[128,1024]{1,0:T(8,128)(2,1)}, f32[512,768]{1,0:T(8,128)}, f32[192,1024]{1,0:T(8,128)}) custom-call(s32[8,128]{1,0:T(8,128)} %bitcast.10, f32[8,128]{1,0:T(8,128)} %bitcast.11, bf16[128,1024]{1,0:T(8,128)(2,1)} %tok_in.1, bf16[128,1024]{1,0:T(8,128)(2,1)} %grad_in.1, bf16[512,768]{1,0:T(8,128)(2,1)} %bitcast.8, bf16[192,1024]{1,0:T(8,128)(2,1)} %bitcast.9), custom_call_target="tpu_custom_call" | custom-call | tf_op jit(solution)/shard_map/pallas_call | solution.py:464
  102.3 1.7 %copy.12 = bf16[128,1024]{1,0:T(8,128)(2,1)} copy(bf16[128,1024]{1,0:T(8,128)(2,1)} %get-tuple-element.12) | data formatting | bytes 524288
  103.9 0.0 copy-start
  103.9 2.7 %copy.13 = f32[1,512,768]{2,1,0:T(8,128)} copy(f32[1,512,768]{2,1,0:T(8,128)} %bitcast.6) | data formatting | bytes 3145728
  106.7 0.0 copy-done
  106.7 0.9 copy.14
Async XLA Ops:
  103.9 2.7 %copy-start = (f32[192,1024]{1,0:T(8,128)S(1)}, f32[192,1024]{1,0:T(8,128)}, u32[]{:S(2)}) copy-start(f32[192,1024]{1,0:T(8,128)} %get-tuple-element.8) | copy-start | bytes 2359300

commit v2 on v1

--- a/solution.py
+++ b/solution.py
@@ -132,9 +132,9 @@
 def fused_kernel(
     expert_count, capacity,
     ids_ref, gates_ref, tok_in, grad_in, win_in, wdn_in,
-    gtok_out, gin_out, gdn_out,
-    data, meta, win, wdn, acc_in, acc_dn, sel, xs, gs, act, dpre, part,
-    sib_in, y_out, y_in, z_out, z_in, gin_send, gin_recv, gdn_send, gdn_recv,
+    z_in, gin_own, gin_recv, gdn_own, gdn_recv,
+    data, meta, win, wdn, acc_dn, sel, xs, gs, act, dpre, part,
+    sib_in, y_out, y_in, z_out, gin_send, gdn_send,
     local_sem, own_send, fwd_send, y_send, sib_send, recv_sem,
     w_send, w_recv, sib_part_send, sib_part_recv, y_part_send, y_part_recv,
     z_part_send, z_part_recv, g_send, g_recv,
@@ -291,6 +291,12 @@
             device_id=(1 - dp, me), device_id_type=MESH)
 
     half_tiles = half_in // tile
+    keep = pltpu.make_async_copy(z_out.at[0], z_in.at[z], local_sem.at[4])
+
+    def grad_in_rows(half, i):
+        columns = pl.ds(pl.multiple_of(half * half_in + i * tile, tile), tile)
+        return contract_first(xs[:, columns], dpre[...]).astype(BF16)
+
     gdn_part = pltpu.make_async_remote_copy(
         src_ref=gdn_send, dst_ref=gdn_recv,
         send_sem=g_send.at[half_tiles], recv_sem=g_recv.at[half_tiles],
@@ -309,22 +315,17 @@
             part[k, c, y].astype(F32) + sib_in[k, y].astype(F32) + y_in[k].astype(F32)
         ).astype(BF16)
 
-        @pl.when(k > 0)
-        def _():
-            z_part(jnp.maximum(k, 1), z).start()
-
-    acc_in[...] = jnp.zeros_like(acc_in)
-    acc_dn[...] = jnp.zeros_like(acc_dn)
+        if k > 0:
+            z_part(k, z).start()
+        else:
+            keep.start()
+
     for k in range(1, min(3, depth)):
         arrivals(k)
     local[2].wait()
     local[3].wait()
 
     def chunk(k, carry):
-        @pl.when((k >= 1) & (k + 2 < depth))
-        def _():
-            arrivals(jnp.minimum(k + 2, depth - 1))
-
         zz = near(k)
         block = block_of(zz, 1 - y, c)
         arrived(block)
@@ -337,7 +338,15 @@
             for copy in weights:
                 copy.wait_recv()
 
+        last = k == depth - 1
+
+        @pl.when(last)
+        def _():
+            for early in range(depth - 2):
+                combine_y(early)
+
         first = zz * 4
+        at_rows = pl.ds(pl.multiple_of(k * slots, 16), slots)
         slot_rows = lax.broadcasted_iota(jnp.int32, (slots, token_rows), 0)
         slot_gate = jnp.zeros((slots, 1), F32)
         for j in range(4):
@@ -351,74 +360,57 @@
             sel[:, j * token_rows : (j + 1) * token_rows] = jnp.where(hit, 1.0, 0.0).astype(BF16)
         chosen = sel[...]
         chunk_tokens = data[pl.ds(first, 4), 0].reshape(4 * token_rows, model_width)
-        xs[...] = jnp.dot(chosen, chunk_tokens, preferred_element_type=F32).astype(BF16)
+        own_tokens = jnp.dot(chosen, chunk_tokens, preferred_element_type=F32).astype(BF16)
+        xs[at_rows, :] = own_tokens
         chunk_grads = data[pl.ds(first, 4), 1].reshape(4 * token_rows, model_width)
-        gs[...] = (
+        own_grads = (
             slot_gate * jnp.dot(chosen, chunk_grads, preferred_element_type=F32)
         ).astype(BF16)
-        preact = jnp.dot(xs[...], win[...], preferred_element_type=F32)
-        grad_hidden = contract_last(gs[...], wdn[...])
-        act[...] = hidden_from(preact)
-        dpre[...] = pre_grads(preact, grad_hidden)
-
-        last = k == depth - 1
-
-        @pl.loop(0, 4)
-        def _(i):
-            at = ((1 - dp) * half_tiles + i) % 4
-            rows = pl.ds(pl.multiple_of(at * tile, tile), tile)
-            total = acc_in[rows, :] + contract_first(xs[:, rows], dpre[...])
-            acc_in[rows, :] = total
-
-            @pl.when(last & (i < half_tiles))
-            def _():
-                piece = jnp.minimum(i, half_tiles - 1)
-                gin_send[pl.ds(pl.multiple_of(piece * tile, tile), tile), :] = total.astype(BF16)
-                gin_part(piece).start()
-
-        acc_dn[...] += contract_first(act[...], gs[...])
+        gs[at_rows, :] = own_grads
+        preact = jnp.dot(xs[at_rows, :], win[...], preferred_element_type=F32)
+        grad_hidden = contract_last(gs[at_rows, :], wdn[...])
+        act[at_rows, :] = hidden_from(preact)
+        dpre[at_rows, :] = pre_grads(preact, grad_hidden)
+
+        @pl.when((k >= 1) & (k + 2 < depth))
+        def _():
+            arrivals(jnp.minimum(k + 2, depth - 1))
 
         @pl.when(last)
         def _():
+            @pl.loop(0, half_tiles)
+            def _(i):
+                gin_send[pl.ds(pl.multiple_of(i * tile, tile), tile), :] = grad_in_rows(1 - dp, i)
+                gin_part(i).start()
+
+            acc_dn[...] = contract_first(act[...], gs[...])
             gdn_send[...] = acc_dn[peer_rows_dn, :].astype(BF16)
             gdn_part.start()
 
-        back = contract_last(dpre[...], win[...]).astype(BF16)
+        back = contract_last(dpre[at_rows, :], win[...]).astype(BF16)
         spread = contract_first(sel[...], back).astype(BF16)
         for j in range(4):
             part[k, j % 2, j // 2] = spread[j * token_rows : (j + 1) * token_rows]
         sib_part(k).start()
-
-        @pl.when(k >= 1)
-        def _():
-            combine_y(jnp.maximum(k - 1, 0))
-
-        @pl.when(k >= 2)
-        def _():
-            combine_z(jnp.maximum(k - 2, 0))
-
         return carry
 
     lax.fori_loop(0, depth, chunk, 0)
+    combine_y(depth - 2)
     combine_y(depth - 1)
-    if depth >= 2:
-        combine_z(jnp.int32(depth - 2))
-    combine_z(jnp.int32(depth - 1))
-
-    total = z_out[0].astype(F32)
+
+    @pl.loop(0, half_tiles)
+    def _(i):
+        gin_own[pl.ds(pl.multiple_of(i * tile, tile), tile), :] = grad_in_rows(dp, i)
+
+    gdn_own[...] = acc_dn[own_rows_dn, :].astype(BF16)
+    for k in range(depth):
+        combine_z(k)
     for step in range(1, depth):
-        slot = (z + step) % depth
-        z_part(step, slot).wait_recv()
-        total = total + z_in[slot].astype(F32)
-    gtok_out[...] = total.astype(BF16)
-
+        z_part(step, (z + step) % depth).wait_recv()
+    keep.wait()
     for i in range(half_tiles):
         gin_part(i).wait_recv()
-        rows = pl.ds(i * tile, tile)
-        own = pl.ds(pl.multiple_of(dp * half_in + i * tile, tile), tile)
-        gin_out[rows, :] = acc_in[own, :].astype(BF16).astype(F32) + gin_recv[rows, :].astype(F32)
     gdn_part.wait_recv()
-    gdn_out[...] = acc_dn[own_rows_dn, :].astype(BF16).astype(F32) + gdn_recv[...].astype(F32)
 
     @pl.when(z > 0)
     def _():
@@ -461,39 +453,43 @@
     half_tiles = half_in // (model_width // 4)
     dma = lambda *shape: pltpu.SemaphoreType.DMA(shape)
     vmem = lambda shape, dtype=BF16: pltpu.VMEM(shape, dtype)
-    grad_tokens, grad_in, grad_down = pl.pallas_call(
+    z_parts, own_in, other_in, own_dn, other_dn = pl.pallas_call(
         functools.partial(fused_kernel, expert_count, capacity),
         out_shape=(
-            jax.ShapeDtypeStruct((token_rows, model_width), BF16),
-            jax.ShapeDtypeStruct((half_in, in_width), F32),
-            jax.ShapeDtypeStruct((half_dn, model_width), F32),
+            jax.ShapeDtypeStruct((depth, token_rows, model_width), BF16),
+            jax.ShapeDtypeStruct((half_in, in_width), BF16),
+            jax.ShapeDtypeStruct((half_in, in_width), BF16),
+            jax.ShapeDtypeStruct((half_dn, model_width), BF16),
+            jax.ShapeDtypeStruct((half_dn, model_width), BF16),
         ),
         in_specs=[pl.BlockSpec(memory_space=pltpu.VMEM)] * 2
         + [pl.BlockSpec(memory_space=pl.ANY)] * 4,
-        out_specs=(pl.BlockSpec(memory_space=pltpu.VMEM),) * 3,
+        out_specs=(
+            pl.BlockSpec(memory_space=pl.ANY),
+            pl.BlockSpec(memory_space=pltpu.VMEM),
+            pl.BlockSpec(memory_space=pl.ANY),
+            pl.BlockSpec(memory_space=pltpu.VMEM),
+            pl.BlockSpec(memory_space=pl.ANY),
+        ),
         scratch_shapes=[
             vmem((expert_count, 2, token_rows, model_width)),
             vmem((expert_count, 2 * expert_count, token_rows), F32),
             vmem((2 * half_in, in_width)),
             vmem((2 * half_dn, model_width)),
-            vmem((2 * half_in, in_width), F32),
             vmem((2 * half_dn, model_width), F32),
             vmem((slots, 4 * token_rows)),
-            vmem((slots, model_width)),
-            vmem((slots, model_width)),
-            vmem((slots, in_width // 2)),
-            vmem((slots, in_width)),
+            vmem((depth * slots, model_width)),
+            vmem((depth * slots, model_width)),
+            vmem((depth * slots, in_width // 2)),
+            vmem((depth * slots, in_width)),
             vmem((depth, 2, 2, token_rows, model_width)),
             vmem((depth, 2, token_rows, model_width)),
             vmem((depth, token_rows, model_width)),
             vmem((depth, token_rows, model_width)),
             vmem((depth, token_rows, model_width)),
-            vmem((depth, token_rows, model_width)),
-            vmem((half_in, in_width)),
             vmem((half_in, in_width)),
             vmem((half_dn, model_width)),
-            vmem((half_dn, model_width)),
-            dma(4), dma(2, 2), dma(depth, 2), dma(depth, 2), dma(depth, 2, 2),
+            dma(5), dma(2, 2), dma(depth, 2), dma(depth, 2), dma(depth, 2, 2),
             dma(expert_count, 2), dma(2), dma(2), dma(depth), dma(depth), dma(depth), dma(depth),
             dma(depth), dma(depth), dma(half_tiles + 1), dma(half_tiles + 1),
         ],
@@ -501,6 +497,9 @@
             collective_id=0, has_side_effects=True, vmem_limit_bytes=VMEM_BYTES
         ),
     )(expert_ids.T, gates.T, tokens, grad_out, w_in[0], w_down[0])
+    grad_tokens = jnp.sum(z_parts.astype(F32), axis=0).astype(BF16)
+    grad_in = own_in.astype(F32) + other_in.astype(F32)
+    grad_down = own_dn.astype(F32) + other_dn.astype(F32)
     return grad_tokens, grad_in[None], grad_down[None]
 
 

time: 108 us -> 109 us (level)
  other arithmetic: 0 us -> 5.71 us
  local copies, waits for them, and re-layouts: 5.28 us -> 0.01 us
    unnamed x5 -> x4, local copies, waits for them, and re-layouts: 5.28 us -> 0.01 us
    broadcast_in_dim x0 -> x2, other arithmetic: none -> 3.41 us  [fused_on_device(): return (grad_tokens, grad_in[None], grad_down[None])]
    reduce_sum x0 -> x1, other arithmetic: none -> 2.3 us  [fused_on_device(): grad_tokens = jnp.sum(z_parts.astype(F32), axis=0).astype(BF16)]
where the time goes in v2:
time: 109 us
  Pallas kernels  102 us (94%)
  other arithmetic  5.71 us (5%)
    pallas_call x1, Pallas kernels, fused_on_device(): pl.pallas_call(functools.partial(fused_kernel, expert_count, capacity), o...  102 us
    broadcast_in_dim x2, other arithmetic, fused_on_device(): return (grad_tokens, grad_in[None], grad_down[None])  3.41 us
    reduce_sum x1, other arithmetic, fused_on_device(): grad_tokens = jnp.sum(z_parts.astype(F32), axis=0).astype(BF16)  2.3 us

profile of v2, /device:TPU:0, one launch (start us, length us, event | category | flops | bytes accessed | tf_op | source)
XLA Modules:
  0.0 108.7 jit_solution(7748344317740197061)
XLA Ops:
  0.6 102.3 %shard_map.85 = (bf16[4,128,1024]{2,1,0:T(8,128)(2,1)}, bf16[512,768]{1,0:T(8,128)(2,1)}, bf16[512,768]{1,0:T(8,128)(2,1)}, bf16[192,1024]{1,0:T(8,128)(2,1)}, bf16[192,1024]{1,0:T(8,128)(2,1)}) custom-call(s32[8,128]{1,0:T(8,128)} %bitcast.10, f32[8,128]{1,0:T(8,128)} %bitcast.11, bf16[128,1024]{1,0:T(8,128)(2,1)} %tok_in.1, bf16[128,1024]{1,0:T(8,128)(2,1)} %grad_in.1, ...), custom_call_target="tpu_custom_call" | custom-call | tf_op jit(solution)/shard_map/pallas_call | solution.py:456
  102.9 0.0 copy-start
  103.0 0.0 copy-start.1
  103.0 2.3 %reduce_sum.12 = bf16[128,1024]{1,0:T(8,128)(2,1)} reduce(bf16[4,128,1024]{2,1,0:T(8,128)(2,1)} %get-tuple-element.8, bf16[]{:T(256)} %constant.2.clone.1), dimensions={0}, to_apply=%region_0.0 | reduce | flops 393216 | bytes 1310722 | tf_op jit(solution)/shard_map/reduce_sum | solution.py:500
  105.3 2.1 %add_bitcast_fusion.1 = f32[1,192,1024]{2,1,0:T(8,128)} fusion(bf16[192,1024]{1,0:T(8,128)(2,1)} %get-tuple-element.12, bf16[192,1024]{1,0:T(8,128)(2,1)} %get-tuple-element.11), kind=kLoop, calls=%fused_computation.1 | loop fusion | flops 589824 | bytes 1572864 | tf_op jit(solution)/shard_map/broadcast_in_dim | solution.py:503
  107.4 0.0 copy-done
  107.4 0.0 copy-done.1
  107.4 1.3 %add_bitcast_fusion = f32[1,512,768]{2,1,0:T(8,128)} fusion(bf16[512,768]{1,0:T(8,128)(2,1)S(1)} %copy-done.1, bf16[512,768]{1,0:T(8,128)(2,1)S(1)} %copy-done), kind=kLoop, calls=%fused_computation | loop fusion | flops 1179648 | bytes 3145728 | tf_op jit(solution)/shard_map/broadcast_in_dim | solution.py:503
Async XLA Ops:
  102.9 4.4 %copy-start = (bf16[512,768]{1,0:T(8,128)(2,1)S(1)}, bf16[512,768]{1,0:T(8,128)(2,1)}, u32[]{:S(2)}) copy-start(bf16[512,768]{1,0:T(8,128)(2,1)} %get-tuple-element.9) | copy-start | bytes 2359300
  103.0 4.4 %copy-start.1 = (bf16[512,768]{1,0:T(8,128)(2,1)S(1)}, bf16[512,768]{1,0:T(8,128)(2,1)}, u32[]{:S(2)}) copy-start(bf16[512,768]{1,0:T(8,128)(2,1)} %get-tuple-element.10) | copy-start | bytes 2359300

commit v3 on v2

--- a/solution.py
+++ b/solution.py
@@ -342,7 +342,7 @@
 
         @pl.when(last)
         def _():
-            for early in range(depth - 2):
+            for early in range(1, depth - 1):
                 combine_y(early)
 
         first = zz * 4
@@ -395,16 +395,18 @@
         return carry
 
     lax.fori_loop(0, depth, chunk, 0)
-    combine_y(depth - 2)
     combine_y(depth - 1)
+    for k in range(1, depth - 1):
+        combine_z(k)
+    combine_y(0)
 
     @pl.loop(0, half_tiles)
     def _(i):
         gin_own[pl.ds(pl.multiple_of(i * tile, tile), tile), :] = grad_in_rows(dp, i)
 
+    combine_z(depth - 1)
     gdn_own[...] = acc_dn[own_rows_dn, :].astype(BF16)
-    for k in range(depth):
-        combine_z(k)
+    combine_z(0)
     for step in range(1, depth):
         z_part(step, (z + step) % depth).wait_recv()
     keep.wait()

time: 109 us -> 106 us (0.972)
  Pallas kernels: 102 us -> 99.6 us
    pallas_call x1, Pallas kernels: 102 us -> 99.6 us  [fused_on_device(): pl.pallas_call(functools.partial(fused_kernel, expert_count, capacity), o...]
where the time goes in v3:
time: 106 us
  Pallas kernels  99.6 us (94%)
  other arithmetic  5.71 us (5%)
    pallas_call x1, Pallas kernels, fused_on_device(): pl.pallas_call(functools.partial(fused_kernel, expert_count, capacity), o...  99.6 us
    broadcast_in_dim x2, other arithmetic, fused_on_device(): return (grad_tokens, grad_in[None], grad_down[None])  3.41 us
    reduce_sum x1, other arithmetic, fused_on_device(): grad_tokens = jnp.sum(z_parts.astype(F32), axis=0).astype(BF16)  2.3 us

profile of v3, /device:TPU:0, one launch (start us, length us, event | category | flops | bytes accessed | tf_op | source)
XLA Modules:
  0.0 106.0 jit_solution(5455657961052422621)
XLA Ops:
  0.6 99.6 %shard_map.85 = (bf16[4,128,1024]{2,1,0:T(8,128)(2,1)}, bf16[512,768]{1,0:T(8,128)(2,1)}, bf16[512,768]{1,0:T(8,128)(2,1)}, bf16[192,1024]{1,0:T(8,128)(2,1)}, bf16[192,1024]{1,0:T(8,128)(2,1)}) custom-call(s32[8,128]{1,0:T(8,128)} %bitcast.10, f32[8,128]{1,0:T(8,128)} %bitcast.11, bf16[128,1024]{1,0:T(8,128)(2,1)} %tok_in.1, bf16[128,1024]{1,0:T(8,128)(2,1)} %grad_in.1, ...), custom_call_target="tpu_custom_call" | custom-call | tf_op jit(solution)/shard_map/pallas_call | solution.py:458
  100.2 0.0 copy-start
  100.3 0.0 copy-start.1
  100.3 2.3 %reduce_sum.12 = bf16[128,1024]{1,0:T(8,128)(2,1)} reduce(bf16[4,128,1024]{2,1,0:T(8,128)(2,1)} %get-tuple-element.8, bf16[]{:T(256)} %constant.2.clone.1), dimensions={0}, to_apply=%region_0.0 | reduce | flops 393216 | bytes 1310722 | tf_op jit(solution)/shard_map/reduce_sum | solution.py:502
  102.6 2.1 %add_bitcast_fusion.1 = f32[1,192,1024]{2,1,0:T(8,128)} fusion(bf16[192,1024]{1,0:T(8,128)(2,1)} %get-tuple-element.12, bf16[192,1024]{1,0:T(8,128)(2,1)} %get-tuple-element.11), kind=kLoop, calls=%fused_computation.1 | loop fusion | flops 589824 | bytes 1572864 | tf_op jit(solution)/shard_map/broadcast_in_dim | solution.py:505
  104.7 0.0 copy-done
  104.7 0.0 copy-done.1
  104.7 1.3 %add_bitcast_fusion = f32[1,512,768]{2,1,0:T(8,128)} fusion(bf16[512,768]{1,0:T(8,128)(2,1)S(1)} %copy-done.1, bf16[512,768]{1,0:T(8,128)(2,1)S(1)} %copy-done), kind=kLoop, calls=%fused_computation | loop fusion | flops 1179648 | bytes 3145728 | tf_op jit(solution)/shard_map/broadcast_in_dim | solution.py:505
Async XLA Ops:
  100.2 4.4 %copy-start = (bf16[512,768]{1,0:T(8,128)(2,1)S(1)}, bf16[512,768]{1,0:T(8,128)(2,1)}, u32[]{:S(2)}) copy-start(bf16[512,768]{1,0:T(8,128)(2,1)} %get-tuple-element.9) | copy-start | bytes 2359300
  100.3 4.4 %copy-start.1 = (bf16[512,768]{1,0:T(8,128)(2,1)S(1)}, bf16[512,768]{1,0:T(8,128)(2,1)}, u32[]{:S(2)}) copy-start(bf16[512,768]{1,0:T(8,128)(2,1)} %get-tuple-element.10) | copy-start | bytes 2359300

commit v4 on v3

--- a/solution.py
+++ b/solution.py
@@ -163,29 +163,24 @@
                 total = total + hit * table[zz][kk]
         return total
 
-    def data_copy(block, target, sems):
-        return (
-            pltpu.make_async_remote_copy(
-                src_ref=data.at[block], dst_ref=data.at[block],
-                send_sem=sems.at[0], recv_sem=recv_sem.at[block, 0],
-                device_id=(dp, target), device_id_type=MESH),
-            pltpu.make_async_remote_copy(
-                src_ref=meta.at[block], dst_ref=meta.at[block],
-                send_sem=sems.at[1], recv_sem=recv_sem.at[block, 1],
-                device_id=(dp, target), device_id_type=MESH),
-        )
+    def data_copy(block, target, sems, piece):
+        ref = meta.at[block] if piece == 2 else data.at[block, piece]
+        return pltpu.make_async_remote_copy(
+            src_ref=ref, dst_ref=ref,
+            send_sem=sems.at[piece], recv_sem=recv_sem.at[block, piece],
+            device_id=(dp, target), device_id_type=MESH)
 
     def ship(block, target, sems):
-        for copy in data_copy(block, target, sems):
-            copy.start()
+        for piece in range(3):
+            data_copy(block, target, sems, piece).start()
 
     def sent(block, target, sems):
-        for copy in data_copy(block, target, sems):
-            copy.wait_send()
+        for piece in range(3):
+            data_copy(block, target, sems, piece).wait_send()
 
     def arrived(block):
-        for copy in data_copy(block, sib, own_send.at[0]):
-            copy.wait_recv()
+        for piece in range(3):
+            data_copy(block, sib, own_send.at[0], piece).wait_recv()
 
     own_rows_in = pl.ds(pl.multiple_of(dp * half_in, 16), half_in)
     own_rows_dn = pl.ds(pl.multiple_of(dp * half_dn, 16), half_dn)
@@ -255,15 +250,16 @@
     def arrivals(k):
         zz = near(k)
         block = block_of(zz, y, c)
-        arrived(block)
         more, step_to = onward(zz)
-
-        @pl.when(more)
-        def _():
-            ship(block, block_of(step_to, y, c), fwd_send.at[k])
-
-        ship(block, y_peer, y_send.at[k])
-        ship(block, sib, sib_send.at[k, 0])
+        for piece in range(3):
+            data_copy(block, sib, own_send.at[0], piece).wait_recv()
+
+            @pl.when(more)
+            def _():
+                data_copy(block, block_of(step_to, y, c), fwd_send.at[k], piece).start()
+
+            data_copy(block, y_peer, y_send.at[k], piece).start()
+            data_copy(block, sib, sib_send.at[k, 0], piece).start()
 
     def sib_part(k):
         return pltpu.make_async_remote_copy(
@@ -322,11 +318,22 @@
 
     for k in range(1, min(3, depth)):
         arrivals(k)
+    at_end = (z == 0) | (z == depth - 1)
+    if depth > 3:
+        @pl.when(~at_end)
+        def _():
+            arrivals(depth - 1)
+
     local[2].wait()
     local[3].wait()
 
     def chunk(k, carry):
         zz = near(k)
+        if depth > 3:
+            @pl.when((k == 1) & at_end)
+            def _():
+                arrivals(depth - 1)
+
         block = block_of(zz, 1 - y, c)
         arrived(block)
         ship(block, sib, sib_send.at[k, 1])
@@ -371,10 +378,6 @@
         grad_hidden = contract_last(gs[at_rows, :], wdn[...])
         act[at_rows, :] = hidden_from(preact)
         dpre[at_rows, :] = pre_grads(preact, grad_hidden)
-
-        @pl.when((k >= 1) & (k + 2 < depth))
-        def _():
-            arrivals(jnp.minimum(k + 2, depth - 1))
 
         @pl.when(last)
         def _():
@@ -491,8 +494,8 @@
             vmem((depth, token_rows, model_width)),
             vmem((half_in, in_width)),
             vmem((half_dn, model_width)),
-            dma(5), dma(2, 2), dma(depth, 2), dma(depth, 2), dma(depth, 2, 2),
-            dma(expert_count, 2), dma(2), dma(2), dma(depth), dma(depth), dma(depth), dma(depth),
+            dma(5), dma(2, 3), dma(depth, 3), dma(depth, 3), dma(depth, 2, 3),
+            dma(expert_count, 3), dma(2), dma(2), dma(depth), dma(depth), dma(depth), dma(depth),
             dma(depth), dma(depth), dma(half_tiles + 1), dma(half_tiles + 1),
         ],
         compiler_params=pltpu.CompilerParams(

time: 106 us -> 98 us (0.925)
  Pallas kernels: 99.6 us -> 90.6 us
    pallas_call x1, Pallas kernels: 99.6 us -> 90.6 us  [fused_on_device(): pl.pallas_call(functools.partial(fused_kernel, expert_count, capacity), o...]
where the time goes in v4:
time: 98 us; the launch traced here: 96.9 us
  Pallas kernels  90.6 us (92%)
  other arithmetic  5.71 us (6%)
    pallas_call x1, Pallas kernels, fused_on_device(): pl.pallas_call(functools.partial(fused_kernel, expert_count, capacity), o...  90.6 us
    broadcast_in_dim x2, other arithmetic, fused_on_device(): return (grad_tokens, grad_in[None], grad_down[None])  3.41 us
    reduce_sum x1, other arithmetic, fused_on_device(): grad_tokens = jnp.sum(z_parts.astype(F32), axis=0).astype(BF16)  2.3 us

profile of v4, /device:TPU:0, one launch (start us, length us, event | category | flops | bytes accessed | tf_op | source)
XLA Modules:
  0.0 96.9 jit_solution(16963904390265725946)
XLA Ops:
  0.6 90.6 %shard_map.85 = (bf16[4,128,1024]{2,1,0:T(8,128)(2,1)}, bf16[512,768]{1,0:T(8,128)(2,1)}, bf16[512,768]{1,0:T(8,128)(2,1)}, bf16[192,1024]{1,0:T(8,128)(2,1)}, bf16[192,1024]{1,0:T(8,128)(2,1)}) custom-call(s32[8,128]{1,0:T(8,128)} %bitcast.10, f32[8,128]{1,0:T(8,128)} %bitcast.11, bf16[128,1024]{1,0:T(8,128)(2,1)} %tok_in.1, bf16[128,1024]{1,0:T(8,128)(2,1)} %grad_in.1, ...), custom_call_target="tpu_custom_call" | custom-call | tf_op jit(solution)/shard_map/pallas_call | solution.py:461
  91.2 0.0 copy-start
  91.2 0.0 copy-start.1
  91.2 2.3 %reduce_sum.12 = bf16[128,1024]{1,0:T(8,128)(2,1)} reduce(bf16[4,128,1024]{2,1,0:T(8,128)(2,1)} %get-tuple-element.8, bf16[]{:T(256)} %constant.2.clone.1), dimensions={0}, to_apply=%region_0.0 | reduce | flops 393216 | bytes 1310722 | tf_op jit(solution)/shard_map/reduce_sum | solution.py:505
  93.5 2.1 %add_bitcast_fusion.1 = f32[1,192,1024]{2,1,0:T(8,128)} fusion(bf16[192,1024]{1,0:T(8,128)(2,1)} %get-tuple-element.12, bf16[192,1024]{1,0:T(8,128)(2,1)} %get-tuple-element.11), kind=kLoop, calls=%fused_computation.1 | loop fusion | flops 589824 | bytes 1572864 | tf_op jit(solution)/shard_map/broadcast_in_dim | solution.py:508
  95.6 0.0 copy-done
  95.6 0.0 copy-done.1
  95.6 1.3 %add_bitcast_fusion = f32[1,512,768]{2,1,0:T(8,128)} fusion(bf16[512,768]{1,0:T(8,128)(2,1)S(1)} %copy-done.1, bf16[512,768]{1,0:T(8,128)(2,1)S(1)} %copy-done), kind=kLoop, calls=%fused_computation | loop fusion | flops 1179648 | bytes 3145728 | tf_op jit(solution)/shard_map/broadcast_in_dim | solution.py:508
Async XLA Ops:
  91.2 4.4 %copy-start = (bf16[512,768]{1,0:T(8,128)(2,1)S(1)}, bf16[512,768]{1,0:T(8,128)(2,1)}, u32[]{:S(2)}) copy-start(bf16[512,768]{1,0:T(8,128)(2,1)} %get-tuple-element.9) | copy-start | bytes 2359300
  91.2 4.4 %copy-start.1 = (bf16[512,768]{1,0:T(8,128)(2,1)S(1)}, bf16[512,768]{1,0:T(8,128)(2,1)}, u32[]{:S(2)}) copy-start(bf16[512,768]{1,0:T(8,128)(2,1)} %get-tuple-element.10) | copy-start | bytes 2359300

commit v5 on v4

--- a/solution.py
+++ b/solution.py
@@ -298,11 +298,14 @@
         send_sem=g_send.at[half_tiles], recv_sem=g_recv.at[half_tiles],
         device_id=(1 - dp, me), device_id_type=MESH)
 
-    def combine_y(k):
+    def sum_y(k):
         sib_part(k).wait_recv()
         y_out[k] = (
             part[k, c, 1 - y].astype(F32) + sib_in[k, 1 - y].astype(F32)
         ).astype(BF16)
+
+    def combine_y(k):
+        sum_y(k)
         y_part(k).start()
 
     def combine_z(k):
@@ -334,9 +337,17 @@
             def _():
                 arrivals(depth - 1)
 
+        last = k == depth - 1
+
+        @pl.when(last)
+        def _():
+            for early in range(1, depth - 1):
+                sum_y(early)
+
         block = block_of(zz, 1 - y, c)
-        arrived(block)
-        ship(block, sib, sib_send.at[k, 1])
+        for piece in range(3):
+            data_copy(block, sib, own_send.at[0], piece).wait_recv()
+            data_copy(block, sib, sib_send.at[k, 1], piece).start()
         arrived(block_of(zz, y, 1 - c))
         arrived(block_of(zz, 1 - y, 1 - c))
 
@@ -345,12 +356,10 @@
             for copy in weights:
                 copy.wait_recv()
 
-        last = k == depth - 1
-
         @pl.when(last)
         def _():
             for early in range(1, depth - 1):
-                combine_y(early)
+                y_part(early).start()
 
         first = zz * 4
         at_rows = pl.ds(pl.multiple_of(k * slots, 16), slots)

time: 98 us -> 97.8 us (level)
  no operation moved by 1% of the time
where the time goes in v5:
time: 97.8 us; the launch traced here: 96.3 us
  Pallas kernels  89.9 us (92%)
  other arithmetic  5.71 us (6%)
    pallas_call x1, Pallas kernels, fused_on_device(): pl.pallas_call(functools.partial(fused_kernel, expert_count, capacity), o...  89.9 us
    broadcast_in_dim x2, other arithmetic, fused_on_device(): return (grad_tokens, grad_in[None], grad_down[None])  3.41 us
    reduce_sum x1, other arithmetic, fused_on_device(): grad_tokens = jnp.sum(z_parts.astype(F32), axis=0).astype(BF16)  2.3 us

profile of v5, /device:TPU:0, one launch (start us, length us, event | category | flops | bytes accessed | tf_op | source)
XLA Modules:
  0.0 96.3 jit_solution(13284838530327922278)
XLA Ops:
  0.6 89.9 %shard_map.85 = (bf16[4,128,1024]{2,1,0:T(8,128)(2,1)}, bf16[512,768]{1,0:T(8,128)(2,1)}, bf16[512,768]{1,0:T(8,128)(2,1)}, bf16[192,1024]{1,0:T(8,128)(2,1)}, bf16[192,1024]{1,0:T(8,128)(2,1)}) custom-call(s32[8,128]{1,0:T(8,128)} %bitcast.10, f32[8,128]{1,0:T(8,128)} %bitcast.11, bf16[128,1024]{1,0:T(8,128)(2,1)} %tok_in.1, bf16[128,1024]{1,0:T(8,128)(2,1)} %grad_in.1, ...), custom_call_target="tpu_custom_call" | custom-call | tf_op jit(solution)/shard_map/pallas_call | solution.py:470
  90.5 0.0 copy-start
  90.5 0.0 copy-start.1
  90.6 2.3 %reduce_sum.12 = bf16[128,1024]{1,0:T(8,128)(2,1)} reduce(bf16[4,128,1024]{2,1,0:T(8,128)(2,1)} %get-tuple-element.8, bf16[]{:T(256)} %constant.2.clone.1), dimensions={0}, to_apply=%region_0.0 | reduce | flops 393216 | bytes 1310722 | tf_op jit(solution)/shard_map/reduce_sum | solution.py:514
  92.9 2.1 %add_bitcast_fusion.1 = f32[1,192,1024]{2,1,0:T(8,128)} fusion(bf16[192,1024]{1,0:T(8,128)(2,1)} %get-tuple-element.12, bf16[192,1024]{1,0:T(8,128)(2,1)} %get-tuple-element.11), kind=kLoop, calls=%fused_computation.1 | loop fusion | flops 589824 | bytes 1572864 | tf_op jit(solution)/shard_map/broadcast_in_dim | solution.py:517
  95.0 0.0 copy-done
  95.0 0.0 copy-done.1
  95.0 1.3 %add_bitcast_fusion = f32[1,512,768]{2,1,0:T(8,128)} fusion(bf16[512,768]{1,0:T(8,128)(2,1)S(1)} %copy-done.1, bf16[512,768]{1,0:T(8,128)(2,1)S(1)} %copy-done), kind=kLoop, calls=%fused_computation | loop fusion | flops 1179648 | bytes 3145728 | tf_op jit(solution)/shard_map/broadcast_in_dim | solution.py:517
Async XLA Ops:
  90.5 4.4 %copy-start = (bf16[512,768]{1,0:T(8,128)(2,1)S(1)}, bf16[512,768]{1,0:T(8,128)(2,1)}, u32[]{:S(2)}) copy-start(bf16[512,768]{1,0:T(8,128)(2,1)} %get-tuple-element.9) | copy-start | bytes 2359300
  90.5 4.4 %copy-start.1 = (bf16[512,768]{1,0:T(8,128)(2,1)S(1)}, bf16[512,768]{1,0:T(8,128)(2,1)}, u32[]{:S(2)}) copy-start(bf16[512,768]{1,0:T(8,128)(2,1)} %get-tuple-element.10) | copy-start | bytes 2359300
